TPU v7x, 256 devices: a whole 4x4x8 slice. The times are simulated.
256 devices in a mesh: tower: 8 (over x, core), peer: 32 (over z, y).
Axes of the slice: x: 4, y: 4, z: 8, core: 2. Of those that a mesh axis runs over, the one named last changes fastest.
Arguments:
- embeddings: bfloat16 [16384, 2048], P('tower', 'peer'), may hold values from -6 to 6
- session_lists: int32 [8, 2048], P('tower'), may hold values from 0 to 2047, each once within a row
- owners: int32 [16384, 1], P(('tower', 'peer')), may hold values from 0 to 7; in each aligned block of 64 rows (0 to 63, 64 to 127, ...) at most 16 rows name the same one
- counts: int32 [16384], P(('tower', 'peer')), may hold values from 1 to 3, as said below
- item_feats: bfloat16 [98304, 256], P(('tower', 'peer')), may hold values from -6 to 6
- cotangent: bfloat16 [98304, 1024], P(('tower', 'peer')), may hold values from -6 to 6
- cross_down: bfloat16 [2048, 256], replicated, may hold values from -0.125 to 0.125
- cross_up: bfloat16 [256, 2048], replicated, may hold values from -0.375 to 0.375
- compress: bfloat16 [2048, 256], replicated, may hold values from -0.125 to 0.125
- over_first: bfloat16 [512, 4096], replicated, may hold values from -0.25 to 0.25
- over_second: bfloat16 [4096, 1024], P('peer'), may hold values from -0.09375 to 0.09375
- over_third: bfloat16 [1024, 1024], replicated, may hold values from -0.1875 to 0.1875
Outputs:
- over_out: bfloat16 [98304, 1024], P(('tower', 'peer'))
- emb_grad: bfloat16 [16384, 2048], P('tower', 'peer')
Inputs may be any that keep to these rules, and one draw needn't show every extreme that they name: `session_lists`: each row is a permutation of the tower's 64 * 32 table rows. `owners`: within the 64 sessions of one device, no tower owns more than 16 of them. `counts`: the first session of every device has 3 samples and the second has one.
All inputs are finite; a program needn't handle non-finite values.
Results may differ from a plain program's by a relative error of at most 0.02.
Values may be sent and summed in bfloat16 or wider, within the bound.
A program may use at most 128 MiB of HBM per device.

v0:
```python
import jax
import jax.numpy as jnp
from jax import lax
from jax.sharding import PartitionSpec as P

MOSTC = 3


def silu_slope(pre):
    sigma = jax.nn.sigmoid(pre)
    return sigma * (1.0 + pre * (1.0 - sigma))


def times_t(left, right):
    return lax.dot_general(
        left, right, (((1,), (1,)), ((), ())), preferred_element_type=jnp.float32
    )


def body(
    embeddings,
    session_lists,
    owners,
    counts,
    item_feats,
    cotangent,
    cross_down,
    cross_up,
    compress,
    over_first,
    over_second,
    over_third,
):
    towers = lax.axis_size("tower")
    comp_width = compress.shape[1]
    grid_rows = item_feats.shape[0]
    slots = grid_rows // (towers * MOSTC)
    order = session_lists[0]
    picked = jnp.take(embeddings, order, axis=0)
    session_rows = lax.all_to_all(picked, "peer", split_axis=0, concat_axis=1, tiled=True)
    low = jnp.dot(session_rows, cross_down, preferred_element_type=jnp.float32).astype(jnp.bfloat16)
    lift = jnp.dot(low, cross_up, preferred_element_type=jnp.float32)
    rows_wide = session_rows.astype(jnp.float32)
    crossed = (rows_wide * lift + rows_wide).astype(jnp.bfloat16)
    compressed = jnp.dot(crossed, compress, preferred_element_type=jnp.float32).astype(jnp.bfloat16)
    owner_list = owners[:, 0]
    choose = (owner_list[:, None] == jnp.arange(towers, dtype=jnp.int32)[None, :]).astype(jnp.int32)
    earlier = jnp.cumsum(choose, axis=0) - choose
    position = jnp.sum(choose * earlier, axis=1)
    target = owner_list * slots + position
    dispatch = (target[:, None] == jnp.arange(towers * slots, dtype=jnp.int32)[None, :]).astype(
        jnp.int32
    )
    dispatch_half = dispatch.astype(jnp.bfloat16)
    send_rows = lax.dot_general(
        dispatch_half, compressed, (((0,), (0,)), ((), ())), preferred_element_type=jnp.float32
    ).astype(jnp.bfloat16)
    send_counts = jnp.sum(dispatch * counts[:, None], axis=0)
    repeated = jnp.broadcast_to(send_rows[:, None, :], (towers * slots, MOSTC, comp_width))
    repeated = repeated.reshape(towers, slots * MOSTC, comp_width)
    got_rows, got_counts = (
        lax.all_to_all(repeated, "tower", split_axis=0, concat_axis=0, tiled=True),
        lax.all_to_all(
            send_counts.reshape(towers, slots), "tower", split_axis=0, concat_axis=0, tiled=True
        ),
    )
    expanded = got_rows.reshape(grid_rows, comp_width)
    live = (
        jnp.arange(MOSTC, dtype=jnp.int32)[None, :] < got_counts.reshape(towers * slots)[:, None]
    ).astype(jnp.float32)
    live = live.reshape(grid_rows)
    inputs = jnp.concatenate([expanded, item_feats], axis=1)
    pre_first = jnp.dot(inputs, over_first, preferred_element_type=jnp.float32)
    hidden_first = jax.nn.silu(pre_first).astype(jnp.bfloat16)
    pre_second = jnp.dot(
        hidden_first,
        lax.all_gather(over_second, "peer", axis=0, tiled=True),
        preferred_element_type=jnp.float32,
    )
    hidden_second = jax.nn.silu(pre_second).astype(jnp.bfloat16)
    over_out = (
        jnp.dot(hidden_second, over_third, preferred_element_type=jnp.float32) * live[:, None]
    ).astype(jnp.bfloat16)
    masked = cotangent * live[:, None].astype(jnp.bfloat16)
    grad_second = (times_t(masked, over_third) * silu_slope(pre_second)).astype(jnp.bfloat16)
    back_first = times_t(grad_second, lax.all_gather(over_second, "peer", axis=0, tiled=True))
    grad_first = (back_first * silu_slope(pre_first)).astype(jnp.bfloat16)
    sample_grad = times_t(grad_first, over_first[:comp_width]).astype(jnp.bfloat16)
    returned = lax.all_to_all(
        sample_grad.reshape(towers, slots * MOSTC, comp_width),
        "tower",
        split_axis=0,
        concat_axis=0,
        tiled=True,
    )
    slot_grad = jnp.sum(
        returned.astype(jnp.float32).reshape(towers * slots, MOSTC, comp_width), axis=1
    ).astype(jnp.bfloat16)
    session_grad = jnp.dot(dispatch_half, slot_grad, preferred_element_type=jnp.float32).astype(
        jnp.bfloat16
    )
    grad_crossed = times_t(session_grad, compress).astype(jnp.bfloat16)
    grad_lift = (grad_crossed.astype(jnp.float32) * rows_wide).astype(jnp.bfloat16)
    grad_low = times_t(grad_lift, cross_up).astype(jnp.bfloat16)
    grad_rows = (
        grad_crossed.astype(jnp.float32) * (lift + 1.0) + times_t(grad_low, cross_down)
    ).astype(jnp.bfloat16)
    columns_back = lax.all_to_all(grad_rows, "peer", split_axis=1, concat_axis=0, tiled=True)
    emb_grad = jnp.zeros_like(embeddings).at[order].set(columns_back)
    return (over_out, emb_grad)


def solution(mesh):
    return jax.shard_map(
        body,
        mesh=mesh,
        in_specs=(
            P("tower", "peer"),
            P("tower", None),
            P(("tower", "peer"), None),
            P(("tower", "peer")),
            P(("tower", "peer"), None),
            P(("tower", "peer"), None),
            P(),
            P(),
            P(),
            P(),
            P("peer", None),
            P(),
        ),
        out_specs=(P(("tower", "peer"), None), P("tower", "peer")),
        check_vma=False,
    )
```

profile of v0, /device:TPU:32, one launch (start us, length us, event | category | flops | bytes accessed | tf_op | source)
XLA Modules:
  0.0 187.4 jit_solution(9144501375350728294)
XLA Ops:
  7.2 0.0 copy-start
  7.2 0.0 all-gather.2.cloned.1.call-start
  7.2 0.7 all-gather.2.cloned.1.call-update
  7.9 0.7 fusion.25
  8.6 0.1 reduce_window_sum.11
  8.7 0.8 select_reduce_fusion.1
  9.6 0.7 fusion.29
  10.2 0.7 select_reduce_fusion
  11.0 0.7 all_to_all.42
  11.7 4.3 %all-to-all-start.2 = ((s32[8,1,16]{2,1,0:T(1,128)}), s32[8,1,16]{2,1,0:T(1,128)S(1)}, u32[]{:S(2)}, u32[]{:S(2)}) async-start(s32[8,1,16]{2,1,0:T(1,128)} %bitcast.8), calls=%async_computation.2 | async-start | bytes 8192 | tf_op jit(solution)/shard_map/all_to_all | solution.py:63
  16.0 1.2 copy.28
  17.2 0.5 broadcast.66
  17.7 1.3 reduce.7
  19.0 0.1 squeeze.6
  19.1 0.7 compare_select_fusion
  19.8 6.2 %gather_fusion = bf16[2048,64]{1,0:T(8,128)(2,1)S(1)} fusion(bf16[2048,64]{1,0:T(8,128)(2,1)S(1)} %copy.28, s32[2048]{0:T(1024)S(1)} %broadcast_clamp_fusion), kind=kCustom, calls=%fused_computation | custom fusion | bytes 532480 | tf_op jit(solution)/shard_map/jit(_take)/gather | solution.py:39
  26.0 0.3 broadcast_select_fusion
  26.3 1.1 reshape.142
  27.4 0.0 all-to-all-done.2
  27.4 11.4 %all-to-all-start = ((bf16[32,2,2048]{2,1,0:T(2,128)(2,1)}), bf16[32,2,2048]{2,1,0:T(2,128)(2,1)S(1)}, u32[]{:S(2)}, u32[]{:S(2)}) async-start(bf16[32,2,2048]{2,1,0:T(2,128)(2,1)} %reshape.142), calls=%async_computation | async-start | bytes 524288 | tf_op jit(solution)/shard_map/all_to_all | solution.py:40
  38.8 0.6 reduce.8
  39.4 0.1 lt.53
  39.5 14.4 %all-to-all-done = bf16[32,2,2048]{2,1,0:T(2,128)(2,1)S(1)} async-done(((bf16[32,2,2048]{2,1,0:T(2,128)(2,1)}), bf16[32,2,2048]{2,1,0:T(2,128)(2,1)S(1)}, u32[]{:S(2)}, u32[]{:S(2)}) %all-to-all-start) | async-done | bytes 262176 | tf_op jit(solution)/shard_map/all_to_all | solution.py:40
  53.9 0.4 reshape.143
  54.3 0.3 copy.29
  54.6 0.5 all_to_all.40
  55.1 0.0 copy-start.1
  55.1 2.4 %fusion.8 = f32[64,2048]{1,0:T(8,128)S(1)} fusion(bf16[256,2048]{1,0:T(8,128)(2,1)} %param.19, bf16[64,2048]{1,0:T(8,128)(2,1)S(1)} %all_to_all.40, bf16[2048,256]{1,0:T(8,128)(2,1)} %param.18), kind=kOutput, calls=%fused_computation.22 | convolution fusion | flops 134234112 | bytes 2883584 | tf_op jit(solution)/shard_map/dot_general | solution.py:42
  57.5 1.7 convolution_convert_fusion.1
  59.2 0.1 broadcast_in_dim.16
  59.2 0.8 reshape.102
  60.1 4.5 %all-to-all-start.1 = ((bf16[8,48,256]{2,1,0:T(8,128)(2,1)}), bf16[8,48,256]{2,1,0:T(8,128)(2,1)S(1)}, u32[]{:S(2)}, u32[]{:S(2)}) async-start(bf16[8,48,256]{2,1,0:T(8,128)(2,1)} %reshape.102), calls=%async_computation.1 | async-start | bytes 393216 | tf_op jit(solution)/shard_map/all_to_all | solution.py:62
  64.6 0.1 fusion.24
  64.7 0.2 reshape.107
  64.9 6.5 %all-to-all-done.1 = bf16[8,48,256]{2,1,0:T(8,128)(2,1)S(1)} async-done(((bf16[8,48,256]{2,1,0:T(8,128)(2,1)}), bf16[8,48,256]{2,1,0:T(8,128)(2,1)S(1)}, u32[]{:S(2)}, u32[]{:S(2)}) %all-to-all-start.1) | async-done | bytes 196640 | tf_op jit(solution)/shard_map/all_to_all | solution.py:62
  71.4 0.0 copy-done.1
  71.4 6.7 %fusion.13 = f32[384,4096]{1,0:T(8,128)} fusion(bf16[512,4096]{1,0:T(8,128)(2,1)} %param.21, bf16[384,256]{1,0:T(8,128)(2,1)S(1)} %copy-done.1, bf16[384,256]{1,0:T(8,128)(2,1)S(1)} %bitcast.39), kind=kOutput, calls=%fused_computation.30 | convolution fusion | flops 1611399168 | bytes 10878976 | tf_op jit(solution)/shard_map/dot_general | solution.py:73
  78.1 34.4 %all-gather.2.cloned.1.call-done = bf16[4096,1024]{1,0:T(8,128)(2,1)} async-done(((bf16[128,1024]{1,0:T(8,128)(2,1)}), bf16[4096,1024]{1,0:T(8,128)(2,1)}) %all-gather.2.cloned.1.call-update) | async-done | bytes 8388624 | tf_op jit(solution)/shard_map/all_gather | solution.py:77
  112.5 0.0 copy-start.2
  112.5 8.1 %fusion = f32[384,1024]{1,0:T(8,128)S(1)} fusion(bf16[4096,1024]{1,0:T(8,128)(2,1)} %all-gather.2.cloned.1.call-done, f32[384,4096]{1,0:T(8,128)} %fusion.13), kind=kOutput, calls=%fused_computation.5 | convolution fusion | flops 3229089792 | bytes 16252928 | tf_op jit(solution)/shard_map/dot_general | solution.py:75
  120.7 0.0 copy-start.3
  120.7 1.2 copy-done.3
  121.8 0.0 copy-done
  121.8 0.0 copy-done.2
  121.8 2.1 %multiply_convert_fusion.3 = bf16[384,1024]{1,0:T(8,128)(2,1)} fusion(f32[384,1024]{1,0:T(8,128)S(1)} %fusion, bf16[1024,1024]{1,0:T(8,128)(2,1)S(1)} %copy-done, bf16[384,1024]{1,0:T(8,128)(2,1)S(1)} %copy-done.2, bf16[384]{0:T(512)(128)(2,1)S(1)} %convert_element_type.100), kind=kOutput, calls=%fused_computation.12 | convolution fusion | flops 809238528 | bytes 5243648 | tf_op jit(solution)/shard_map/dot_general | solution.py:15
  124.0 10.5 %fusion.5 = bf16[384,256]{1,0:T(8,128)(2,1)S(1)} fusion(bf16[512,4096]{1,0:T(8,128)(2,1)} %param.21, f32[384,4096]{1,0:T(8,128)} %fusion.13, bf16[384,1024]{1,0:T(8,128)(2,1)} %multiply_convert_fusion.3, bf16[4096,1024]{1,0:T(8,128)(2,1)} %all-gather.2.cloned.1.call-done), kind=kOutput, calls=%fused_computation.16 | convolution fusion | flops 4040785920 | bytes 17760256 | tf_op jit(solution)/shard_map/dot_general | solution.py:15
  134.5 10.9 %all_to_all.54 = bf16[8,48,256]{2,1,0:T(8,128)(2,1)S(1)} all-to-all(bf16[8,48,256]{2,1,0:T(8,128)(2,1)S(1)} %bitcast.41), channel_id=1, replica_groups=mesh['tower'=8,'peer'=32] {'tower'}, dimensions={0} | all-to-all | bytes 393216 | tf_op jit(solution)/shard_map/all_to_all | solution.py:89
  145.4 0.1 reshape.105
  145.5 0.3 reduce
  145.9 1.8 fusion.2
  147.6 3.5 %fusion.1 = bf16[64,2048]{1,0:T(8,128)(2,1)} fusion(bf16[2048,256]{1,0:T(8,128)(2,1)} %param.18, bf16[256,2048]{1,0:T(8,128)(2,1)} %param.19, f32[64,2048]{1,0:T(8,128)S(1)} %fusion.2, f32[64,2048]{1,0:T(8,128)S(1)} %fusion.8, bf16[64,2048]{1,0:T(8,128)(2,1)S(1)} %all_to_all.40), kind=kOutput, calls=%fused_computation.7 | convolution fusion | flops 135151616 | bytes 3670016 | tf_op jit(solution)/shard_map/dot_general | solution.py:15
  151.2 1.5 all_to_all.45
  152.6 0.2 copy.34
  152.8 1.1 reshape.144
  153.9 7.6 %all-to-all-start.4 = ((bf16[32,2,2048]{2,1,0:T(2,128)(2,1)}), bf16[32,2,2048]{2,1,0:T(2,128)(2,1)S(1)}, u32[]{:S(2)}, u32[]{:S(2)}) async-start(bf16[32,2,2048]{2,1,0:T(2,128)(2,1)} %reshape.144), calls=%async_computation.4 | async-start | bytes 524288 | tf_op jit(solution)/shard_map/all_to_all | solution.py:108
  161.6 3.3 %multiply_convert_fusion.4 = bf16[384,1024]{1,0:T(8,128)(2,1)} fusion(bf16[1024,1024]{1,0:T(8,128)(2,1)S(1)} %copy-done, f32[384,1024]{1,0:T(8,128)} %copy-done.3, f32[384]{0:T(512)S(1)} %reshape.107), kind=kOutput, calls=%fused_computation.13 | convolution fusion | flops 808058880 | bytes 4457984 | tf_op jit(solution)/shard_map/dot_general | solution.py:82
  164.9 8.5 %all-to-all-done.4 = bf16[32,2,2048]{2,1,0:T(2,128)(2,1)S(1)} async-done(((bf16[32,2,2048]{2,1,0:T(2,128)(2,1)}), bf16[32,2,2048]{2,1,0:T(2,128)(2,1)S(1)}, u32[]{:S(2)}, u32[]{:S(2)}) %all-to-all-start.4) | async-done | bytes 262176 | tf_op jit(solution)/shard_map/all_to_all | solution.py:108
  173.4 0.4 reshape.145
  173.8 5.9 %scatter_custom_fusion = bf16[2048,64]{1,0:T(8,128)(2,1)S(1)} fusion(s32[2048]{0:T(1024)S(1)} %bitcast.43, bf16[2048,64]{1,0:T(8,128)(2,1)S(1)} %bitcast.40, bf16[]{:T(256)} %constant.36.clone.1), kind=kCustom, calls=%fused_computation.35 | custom fusion | bytes 262146 | tf_op jit(solution)/shard_map/scatter | solution.py:109
  179.6 0.9 copy.32
  (3 shorter events, 0.0 us)
Async XLA Ops:
  7.2 114.7 %copy-start = (bf16[1024,1024]{1,0:T(8,128)(2,1)S(1)}, bf16[1024,1024]{1,0:T(8,128)(2,1)}, u32[]{:S(2)}) copy-start(bf16[1024,1024]{1,0:T(8,128)(2,1)} %param.23) | copy-start | bytes 6291460
  7.2 105.4 %all-gather.2.cloned.1.call-start = ((), (), s32[]{:S(2)}) async-start(), calls=%async_computation.5 | async-start | bytes 8650752 | tf_op jit(solution)/shard_map/all_gather | solution.py:77
  11.7 15.8 %all-to-all-start.2 = ((s32[8,1,16]{2,1,0:T(1,128)}), s32[8,1,16]{2,1,0:T(1,128)S(1)}, u32[]{:S(2)}, u32[]{:S(2)}) async-start(s32[8,1,16]{2,1,0:T(1,128)} %bitcast.8), calls=%async_computation.2 | async-start | bytes 8192 | tf_op jit(solution)/shard_map/all_to_all | solution.py:63
  27.4 26.5 %all-to-all-start = ((bf16[32,2,2048]{2,1,0:T(2,128)(2,1)}), bf16[32,2,2048]{2,1,0:T(2,128)(2,1)S(1)}, u32[]{:S(2)}, u32[]{:S(2)}) async-start(bf16[32,2,2048]{2,1,0:T(2,128)(2,1)} %reshape.142), calls=%async_computation | async-start | bytes 524288 | tf_op jit(solution)/shard_map/all_to_all | solution.py:40
  55.1 16.3 %copy-start.1 = (bf16[384,256]{1,0:T(8,128)(2,1)S(1)}, bf16[384,256]{1,0:T(8,128)(2,1)}, u32[]{:S(2)}) copy-start(bf16[384,256]{1,0:T(8,128)(2,1)} %param.16) | copy-start | bytes 589828
  60.1 11.3 %all-to-all-start.1 = ((bf16[8,48,256]{2,1,0:T(8,128)(2,1)}), bf16[8,48,256]{2,1,0:T(8,128)(2,1)S(1)}, u32[]{:S(2)}, u32[]{:S(2)}) async-start(bf16[8,48,256]{2,1,0:T(8,128)(2,1)} %reshape.102), calls=%async_computation.1 | async-start | bytes 393216 | tf_op jit(solution)/shard_map/all_to_all | solution.py:62
  112.5 9.3 %copy-start.2 = (bf16[384,1024]{1,0:T(8,128)(2,1)S(1)}, bf16[384,1024]{1,0:T(8,128)(2,1)}, u32[]{:S(2)}) copy-start(bf16[384,1024]{1,0:T(8,128)(2,1)} %param.17) | copy-start | bytes 2359300
  120.7 1.2 copy-start.3
  153.9 19.5 %all-to-all-start.4 = ((bf16[32,2,2048]{2,1,0:T(2,128)(2,1)}), bf16[32,2,2048]{2,1,0:T(2,128)(2,1)S(1)}, u32[]{:S(2)}, u32[]{:S(2)}) async-start(bf16[32,2,2048]{2,1,0:T(2,128)(2,1)} %reshape.144), calls=%async_computation.4 | async-start | bytes 524288 | tf_op jit(solution)/shard_map/all_to_all | solution.py:108
Sparse Core Ops, SparseCore 0:
  10.6 101.8 all-gather.1
where the time goes:
time: 188 us; the launch traced here: 187 us
  waiting for transfers between devices  64.6 us (34%)
  matrix products  40.1 us (21%)
  starting transfers between devices  27.8 us (15%)
  local copies, waits for them, and re-layouts  23.3 us (12%)
  between operations  14.2 us (8%)
  blocking collectives  10.9 us (6%)
  other arithmetic  6.42 us (3%)
    all_gather x1, waiting for transfers between devices, body(): lax.all_gather(over_second, 'peer', axis=0, tiled=True)  34.4 us
    dot_general x4, matrix products, times_t(): lax.dot_general(left, right, (((1,), (1,)), ((), ())), preferred_element_...  18 us
    all_to_all x1, waiting for transfers between devices, body(): lax.all_to_all(picked, 'peer', split_axis=0, concat_axis=1, tiled=True)  14.4 us
    all_to_all x1, starting transfers between devices, body(): lax.all_to_all(picked, 'peer', split_axis=0, concat_axis=1, tiled=True)  11.4 us
    all_to_all x1, blocking collectives, body(): lax.all_to_all(sample_grad.reshape(towers, slots * MOSTC, comp_width), 't...  10.9 us
    all_to_all x1, waiting for transfers between devices, body(): lax.all_to_all(grad_rows, 'peer', split_axis=1, concat_axis=0, tiled=True)  8.52 us
    dot_general x1, matrix products, body(): jnp.dot(hidden_first, lax.all_gather(over_second, 'peer', axis=0, tiled=T...  8.1 us
    all_to_all x1, starting transfers between devices, body(): lax.all_to_all(grad_rows, 'peer', split_axis=1, concat_axis=0, tiled=True)  7.63 us
  transfers between devices with their start and end apart: 5, of which 4 were waited for; matrix products, arithmetic and copies ran while one was open for 17% of the time, Pallas kernels for 0%

commit v1 on v0

--- a/solution.py
+++ b/solution.py
@@ -105,7 +105,12 @@
     grad_rows = (
         grad_crossed.astype(jnp.float32) * (lift + 1.0) + times_t(grad_low, cross_down)
     ).astype(jnp.bfloat16)
-    columns_back = lax.all_to_all(grad_rows, "peer", split_axis=1, concat_axis=0, tiled=True)
+    columns_back = jnp.concatenate(
+        lax.all_to_all(
+            jnp.stack(jnp.split(grad_rows, lax.axis_size("peer"), axis=1)), "peer", 0, 0
+        ),
+        axis=0,
+    )
     emb_grad = jnp.zeros_like(embeddings).at[order].set(columns_back)
     return (over_out, emb_grad)
 

time: 188 us -> 189 us (level)
    unnamed x15 -> x46, local copies, waits for them, and re-layouts: 6.71 us -> 8.22 us
where the time goes in v1:
time: 189 us; the launch traced here: 188 us
  waiting for transfers between devices  64.6 us (34%)
  matrix products  40.5 us (21%)
  starting transfers between devices  27.8 us (15%)
  local copies, waits for them, and re-layouts  23.2 us (12%)
  between operations  14.3 us (8%)
  blocking collectives  10.9 us (6%)
  other arithmetic  6.42 us (3%)
    all_gather x1, waiting for transfers between devices, body(): lax.all_gather(over_second, 'peer', axis=0, tiled=True)  34.4 us
    dot_general x4, matrix products, times_t(): lax.dot_general(left, right, (((1,), (1,)), ((), ())), preferred_element_...  18.4 us
    all_to_all x1, waiting for transfers between devices, body(): lax.all_to_all(picked, 'peer', split_axis=0, concat_axis=1, tiled=True)  14.4 us
    all_to_all x1, starting transfers between devices, body(): lax.all_to_all(picked, 'peer', split_axis=0, concat_axis=1, tiled=True)  11.4 us
    all_to_all x1, blocking collectives, body(): lax.all_to_all(sample_grad.reshape(towers, slots * MOSTC, comp_width), 't...  10.9 us
    all_to_all x1, waiting for transfers between devices, body(): lax.all_to_all(jnp.stack(jnp.split(grad_rows, lax.axis_size('peer'), axis...  8.52 us
    unnamed x46, local copies, waits for them, and re-layouts  8.22 us
    dot_general x1, matrix products, body(): jnp.dot(hidden_first, lax.all_gather(over_second, 'peer', axis=0, tiled=T...  8.1 us
  transfers between devices with their start and end apart: 5, of which 4 were waited for; matrix products, arithmetic and copies ran while one was open for 17% of the time, Pallas kernels for 0%

profile of v1, /device:TPU:32, one launch (start us, length us, event | category | flops | bytes accessed | tf_op | source)
XLA Modules:
  0.0 187.8 jit_solution(4362244052475032133)
XLA Ops:
  7.2 0.7 all-gather.2.cloned.1.call-update
  7.9 0.7 fusion.25
  8.6 0.1 reduce_window_sum.11
  8.7 0.8 select_reduce_fusion.1
  9.6 0.7 fusion.29
  10.2 0.7 select_reduce_fusion
  11.0 0.7 all_to_all.31
  11.7 4.3 %all-to-all-start.2 = ((s32[8,1,16]{2,1,0:T(1,128)}), s32[8,1,16]{2,1,0:T(1,128)S(1)}, u32[]{:S(2)}, u32[]{:S(2)}) async-start(s32[8,1,16]{2,1,0:T(1,128)} %bitcast.8), calls=%async_computation.2 | async-start | bytes 8192 | tf_op jit(solution)/shard_map/all_to_all | solution.py:63
  16.0 1.2 copy.26
  17.2 0.5 broadcast.66
  17.7 1.3 reduce.7
  19.0 0.1 squeeze.6
  19.1 0.7 compare_select_fusion
  19.8 6.2 %gather_fusion = bf16[2048,64]{1,0:T(8,128)(2,1)S(1)} fusion(bf16[2048,64]{1,0:T(8,128)(2,1)S(1)} %copy.26, s32[2048]{0:T(1024)S(1)} %broadcast_clamp_fusion), kind=kCustom, calls=%fused_computation | custom fusion | bytes 532480 | tf_op jit(solution)/shard_map/jit(_take)/gather | solution.py:39
  26.0 0.3 broadcast_select_fusion
  26.3 1.1 reshape.143
  27.4 11.4 %all-to-all-start = ((bf16[32,2,2048]{2,1,0:T(2,128)(2,1)}), bf16[32,2,2048]{2,1,0:T(2,128)(2,1)S(1)}, u32[]{:S(2)}, u32[]{:S(2)}) async-start(bf16[32,2,2048]{2,1,0:T(2,128)(2,1)} %reshape.143), calls=%async_computation | async-start | bytes 524288 | tf_op jit(solution)/shard_map/all_to_all | solution.py:40
  38.8 0.6 reduce.8
  39.4 0.1 lt.53
  39.5 14.4 %all-to-all-done = bf16[32,2,2048]{2,1,0:T(2,128)(2,1)S(1)} async-done(((bf16[32,2,2048]{2,1,0:T(2,128)(2,1)}), bf16[32,2,2048]{2,1,0:T(2,128)(2,1)S(1)}, u32[]{:S(2)}, u32[]{:S(2)}) %all-to-all-start) | async-done | bytes 262176 | tf_op jit(solution)/shard_map/all_to_all | solution.py:40
  53.9 0.4 reshape.144
  54.3 0.3 copy.27
  54.6 0.5 all_to_all.29
  55.1 2.4 %fusion.8 = f32[64,2048]{1,0:T(8,128)S(1)} fusion(bf16[256,2048]{1,0:T(8,128)(2,1)} %param.19, bf16[64,2048]{1,0:T(8,128)(2,1)S(1)} %all_to_all.29, bf16[2048,256]{1,0:T(8,128)(2,1)} %param.18), kind=kOutput, calls=%fused_computation.22 | convolution fusion | flops 134234112 | bytes 2883584 | tf_op jit(solution)/shard_map/dot_general | solution.py:42
  57.5 1.7 convolution_convert_fusion.1
  59.2 0.8 reshape.102
  60.1 4.5 %all-to-all-start.1 = ((bf16[8,48,256]{2,1,0:T(8,128)(2,1)}), bf16[8,48,256]{2,1,0:T(8,128)(2,1)S(1)}, u32[]{:S(2)}, u32[]{:S(2)}) async-start(bf16[8,48,256]{2,1,0:T(8,128)(2,1)} %reshape.102), calls=%async_computation.1 | async-start | bytes 393216 | tf_op jit(solution)/shard_map/all_to_all | solution.py:62
  64.6 0.1 fusion.24
  64.7 0.2 reshape.108
  64.9 6.5 %all-to-all-done.1 = bf16[8,48,256]{2,1,0:T(8,128)(2,1)S(1)} async-done(((bf16[8,48,256]{2,1,0:T(8,128)(2,1)}), bf16[8,48,256]{2,1,0:T(8,128)(2,1)S(1)}, u32[]{:S(2)}, u32[]{:S(2)}) %all-to-all-start.1) | async-done | bytes 196640 | tf_op jit(solution)/shard_map/all_to_all | solution.py:62
  71.4 6.7 %fusion.13 = f32[384,4096]{1,0:T(8,128)} fusion(bf16[512,4096]{1,0:T(8,128)(2,1)} %param.21, bf16[384,256]{1,0:T(8,128)(2,1)S(1)} %copy-done.1, bf16[384,256]{1,0:T(8,128)(2,1)S(1)} %bitcast.160), kind=kOutput, calls=%fused_computation.30 | convolution fusion | flops 1611399168 | bytes 10878976 | tf_op jit(solution)/shard_map/dot_general | solution.py:73
  78.1 34.4 %all-gather.2.cloned.1.call-done = bf16[4096,1024]{1,0:T(8,128)(2,1)} async-done(((bf16[128,1024]{1,0:T(8,128)(2,1)}), bf16[4096,1024]{1,0:T(8,128)(2,1)}) %all-gather.2.cloned.1.call-update) | async-done | bytes 8388624 | tf_op jit(solution)/shard_map/all_gather | solution.py:77
  112.5 8.1 %fusion = f32[384,1024]{1,0:T(8,128)S(1)} fusion(bf16[4096,1024]{1,0:T(8,128)(2,1)} %all-gather.2.cloned.1.call-done, f32[384,4096]{1,0:T(8,128)} %fusion.13), kind=kOutput, calls=%fused_computation.5 | convolution fusion | flops 3229089792 | bytes 16252928 | tf_op jit(solution)/shard_map/dot_general | solution.py:75
  120.7 1.2 copy-done.3
  121.8 2.1 %multiply_convert_fusion.3 = bf16[384,1024]{1,0:T(8,128)(2,1)} fusion(f32[384,1024]{1,0:T(8,128)S(1)} %fusion, bf16[1024,1024]{1,0:T(8,128)(2,1)S(1)} %copy-done, bf16[384,1024]{1,0:T(8,128)(2,1)S(1)} %copy-done.2, bf16[384]{0:T(512)(128)(2,1)S(1)} %convert_element_type.100), kind=kOutput, calls=%fused_computation.12 | convolution fusion | flops 809238528 | bytes 5243648 | tf_op jit(solution)/shard_map/dot_general | solution.py:15
  124.0 10.5 %fusion.5 = bf16[384,256]{1,0:T(8,128)(2,1)S(1)} fusion(bf16[512,4096]{1,0:T(8,128)(2,1)} %param.21, f32[384,4096]{1,0:T(8,128)} %fusion.13, bf16[384,1024]{1,0:T(8,128)(2,1)} %multiply_convert_fusion.3, bf16[4096,1024]{1,0:T(8,128)(2,1)} %all-gather.2.cloned.1.call-done), kind=kOutput, calls=%fused_computation.16 | convolution fusion | flops 4040785920 | bytes 17760256 | tf_op jit(solution)/shard_map/dot_general | solution.py:15
  134.5 10.9 %all_to_all.40 = bf16[8,48,256]{2,1,0:T(8,128)(2,1)S(1)} all-to-all(bf16[8,48,256]{2,1,0:T(8,128)(2,1)S(1)} %bitcast.162), channel_id=1, replica_groups=mesh['tower'=8,'peer'=32] {'tower'}, dimensions={0} | all-to-all | bytes 393216 | tf_op jit(solution)/shard_map/all_to_all | solution.py:89
  145.4 0.1 reshape.105
  145.5 0.3 reduce
  145.9 2.6 %fusion.2 = f32[64,2048]{1,0:T(8,128)} fusion(bf16[2048,256]{1,0:T(8,128)(2,1)} %param.20, bf16[128,256]{1,0:T(8,128)(2,1)S(1)} %reduce, s32[64]{0:T(128)S(1)} %fusion.29), kind=kOutput, calls=%fused_computation.9 | convolution fusion | flops 71606272 | bytes 1638656 | tf_op jit(solution)/shard_map/dot_general | solution.py:15
  148.4 3.1 %fusion.1 = bf16[64,2048]{1,0:T(8,128)(2,1)S(1)} fusion(bf16[2048,256]{1,0:T(8,128)(2,1)} %param.18, bf16[256,2048]{1,0:T(8,128)(2,1)} %param.19, f32[64,2048]{1,0:T(8,128)} %fusion.2, f32[64,2048]{1,0:T(8,128)S(1)} %fusion.8, bf16[64,2048]{1,0:T(8,128)(2,1)S(1)} %all_to_all.29), kind=kOutput, calls=%fused_computation.7 | convolution fusion | flops 135151616 | bytes 3670016 | tf_op jit(solution)/shard_map/dot_general | solution.py:15
  151.6 0.1 constant_dynamic-update-slice_fusion.30
  151.7 0.1 constant_dynamic-update-slice_fusion.28
  151.8 0.1 constant_dynamic-update-slice_fusion.26
  151.9 0.1 constant_dynamic-update-slice_fusion.24
  152.0 0.1 constant_dynamic-update-slice_fusion.22
  152.1 0.1 constant_dynamic-update-slice_fusion.20
  152.2 0.1 constant_dynamic-update-slice_fusion.18
  152.3 0.1 constant_dynamic-update-slice_fusion.16
  152.4 0.1 constant_dynamic-update-slice_fusion.14
  152.5 0.1 constant_dynamic-update-slice_fusion.12
  152.6 0.1 constant_dynamic-update-slice_fusion.10
  152.7 0.1 constant_dynamic-update-slice_fusion.8
  152.8 0.1 constant_dynamic-update-slice_fusion.6
  152.9 0.1 constant_dynamic-update-slice_fusion.4
  153.0 0.1 constant_dynamic-update-slice_fusion.2
  153.1 0.1 constant_dynamic-update-slice_fusion
  153.2 1.1 reshape.145
  154.3 7.6 %all-to-all-start.4 = ((bf16[32,2,2048]{2,1,0:T(2,128)(2,1)}), bf16[32,2,2048]{2,1,0:T(2,128)(2,1)S(1)}, u32[]{:S(2)}, u32[]{:S(2)}) async-start(bf16[32,2,2048]{2,1,0:T(2,128)(2,1)} %reshape.145), calls=%async_computation.4 | async-start | bytes 524288 | tf_op jit(solution)/shard_map/all_to_all | solution.py:109
  162.0 3.3 %multiply_convert_fusion.4 = bf16[384,1024]{1,0:T(8,128)(2,1)} fusion(bf16[1024,1024]{1,0:T(8,128)(2,1)S(1)} %copy-done, f32[384,1024]{1,0:T(8,128)} %copy-done.3, f32[384]{0:T(512)S(1)} %reshape.108), kind=kOutput, calls=%fused_computation.13 | convolution fusion | flops 808058880 | bytes 4457984 | tf_op jit(solution)/shard_map/dot_general | solution.py:82
  165.3 8.5 %all-to-all-done.4 = bf16[32,2,2048]{2,1,0:T(2,128)(2,1)S(1)} async-done(((bf16[32,2,2048]{2,1,0:T(2,128)(2,1)}), bf16[32,2,2048]{2,1,0:T(2,128)(2,1)S(1)}, u32[]{:S(2)}, u32[]{:S(2)}) %all-to-all-start.4) | async-done | bytes 262176 | tf_op jit(solution)/shard_map/all_to_all | solution.py:109
  173.8 0.4 reshape.146
  174.2 5.9 %scatter_custom_fusion = bf16[2048,64]{1,0:T(8,128)(2,1)S(1)} fusion(s32[2048]{0:T(1024)S(1)} %bitcast.164, bf16[2048,64]{1,0:T(8,128)(2,1)S(1)} %bitcast.161, bf16[]{:T(256)} %constant.36.clone.1), kind=kCustom, calls=%fused_computation.35 | custom fusion | bytes 262146 | tf_op jit(solution)/shard_map/scatter | solution.py:114
  180.0 0.9 copy.29
  (29 shorter events, 0.4 us)
Async XLA Ops:
  7.2 114.7 %copy-start = (bf16[1024,1024]{1,0:T(8,128)(2,1)S(1)}, bf16[1024,1024]{1,0:T(8,128)(2,1)}, u32[]{:S(2)}) copy-start(bf16[1024,1024]{1,0:T(8,128)(2,1)} %param.23) | copy-start | bytes 6291460
  7.2 105.4 %all-gather.2.cloned.1.call-start = ((), (), s32[]{:S(2)}) async-start(), calls=%async_computation.5 | async-start | bytes 8650752 | tf_op jit(solution)/shard_map/all_gather | solution.py:77
  11.7 15.8 %all-to-all-start.2 = ((s32[8,1,16]{2,1,0:T(1,128)}), s32[8,1,16]{2,1,0:T(1,128)S(1)}, u32[]{:S(2)}, u32[]{:S(2)}) async-start(s32[8,1,16]{2,1,0:T(1,128)} %bitcast.8), calls=%async_computation.2 | async-start | bytes 8192 | tf_op jit(solution)/shard_map/all_to_all | solution.py:63
  27.4 26.5 %all-to-all-start = ((bf16[32,2,2048]{2,1,0:T(2,128)(2,1)}), bf16[32,2,2048]{2,1,0:T(2,128)(2,1)S(1)}, u32[]{:S(2)}, u32[]{:S(2)}) async-start(bf16[32,2,2048]{2,1,0:T(2,128)(2,1)} %reshape.143), calls=%async_computation | async-start | bytes 524288 | tf_op jit(solution)/shard_map/all_to_all | solution.py:40
  55.1 16.3 %copy-start.1 = (bf16[384,256]{1,0:T(8,128)(2,1)S(1)}, bf16[384,256]{1,0:T(8,128)(2,1)}, u32[]{:S(2)}) copy-start(bf16[384,256]{1,0:T(8,128)(2,1)} %param.16) | copy-start | bytes 589828
  60.1 11.3 %all-to-all-start.1 = ((bf16[8,48,256]{2,1,0:T(8,128)(2,1)}), bf16[8,48,256]{2,1,0:T(8,128)(2,1)S(1)}, u32[]{:S(2)}, u32[]{:S(2)}) async-start(bf16[8,48,256]{2,1,0:T(8,128)(2,1)} %reshape.102), calls=%async_computation.1 | async-start | bytes 393216 | tf_op jit(solution)/shard_map/all_to_all | solution.py:62
  112.5 9.3 %copy-start.2 = (bf16[384,1024]{1,0:T(8,128)(2,1)S(1)}, bf16[384,1024]{1,0:T(8,128)(2,1)}, u32[]{:S(2)}) copy-start(bf16[384,1024]{1,0:T(8,128)(2,1)} %param.17) | copy-start | bytes 2359300
  120.7 1.2 copy-start.3
  154.3 19.5 %all-to-all-start.4 = ((bf16[32,2,2048]{2,1,0:T(2,128)(2,1)}), bf16[32,2,2048]{2,1,0:T(2,128)(2,1)S(1)}, u32[]{:S(2)}, u32[]{:S(2)}) async-start(bf16[32,2,2048]{2,1,0:T(2,128)(2,1)} %reshape.145), calls=%async_computation.4 | async-start | bytes 524288 | tf_op jit(solution)/shard_map/all_to_all | solution.py:109
Sparse Core Ops, SparseCore 0:
  10.6 101.8 all-gather.1
